TPU v7x, 512 devices: a whole 4x8x8 slice. The times are simulated.
512 devices in a mesh: bead: 8 (over z_hi, x), space: 64 (over y, z_lo, core).
Axes of the slice: x: 4, y: 8, z: 8 (z_hi: 2, z_lo: 4; z = z_hi * 4 + z_lo), core: 2. Of those that a mesh axis runs over, the one named last changes fastest.
Arguments:
- positions: float32 [32, 3, 24576], P('bead', None, 'space'), as said below
- charges: float32 [24576], P('space'), may hold values from -3 to 3
- polar: float32 [24576], P('space'), may hold values from 0.4 to 1.6
- molecule: int32 [24576], P('space'), may hold values from 0 to 8191, as said below
Outputs:
- total_field: float32 [32, 3, 24576], P('bead', None, 'space')
- dipoles: float32 [4, 3, 24576], P(None, None, 'space')
Inputs may be any that keep to these rules, and one draw needn't show every extreme that they name: Each molecule has three atoms, all in one slab block of 384 atoms; no id appears in two blocks. `positions`: in slab block d every atom's first coordinate lies between 15.2 d and 15.2 (d + 1).
All inputs are finite; a program needn't handle non-finite values.
Results may differ from a plain program's by a relative error of at most 0.0003.
Values sent between devices are 32-bit elements; how exact they have to be, the bound alone decides.
A program may use at most 64 MiB of HBM per device.

v0:
```python
import jax
import jax.numpy as jnp
from jax import lax
from jax.sharding import PartitionSpec as P

BEADS = 32
CONTR = 4
ITERS = 2


CUTOFF = 9.0


def padded(block, sides, width):
    for axis, dim in sides:
        count = lax.axis_size(axis)
        forward = [(i, i + 1) for i in range(count - 1)]
        backward = [(target, source) for source, target in forward]
        low = lax.ppermute(
            lax.slice_in_dim(block, block.shape[dim] - width, None, axis=dim), axis, forward
        )
        high = lax.ppermute(lax.slice_in_dim(block, 0, width, axis=dim), axis, backward)
        block = jnp.concatenate([low, block, high], axis=dim)
    return block


def copy_for_each(x, axis):
    copies = jnp.broadcast_to(x, (lax.axis_size(axis), *x.shape))
    return lax.all_to_all(copies, axis, split_axis=0, concat_axis=0, tiled=True)


def of_everyone(x, axis):
    everything = copy_for_each(x, axis)
    return jnp.sum(everything, axis=0)


def pair_field(
    target,
    target_alpha,
    target_mol,
    source,
    source_charge,
    source_alpha,
    source_dip,
    source_mol,
    dipolar,
):
    width = source.shape[1] // 18
    count = source.shape[1] // width
    blocks = (
        source.reshape(3, count, width).transpose(1, 0, 2),
        source_charge.reshape(count, width),
        source_alpha.reshape(count, width),
        source_dip.reshape(3, count, width).transpose(1, 0, 2),
        source_mol.reshape(count, width),
    )

    def step(total, block):
        spot, charge, alpha, dip, mol = block
        diff = target[:, :, None] - spot[:, None, :]
        dist2 = jnp.sum(diff * diff, axis=0)
        keep = (
            (alpha[None, :] > 0.0)
            & (target_mol[:, None] != mol[None, :])
            & (dist2 < CUTOFF * CUTOFF)
        )
        safe2 = jnp.where(keep, dist2, 1.0)
        inverse = lax.rsqrt(safe2)
        inv3 = inverse * inverse * inverse
        both = jnp.where(keep, target_alpha[:, None] * alpha[None, :], 1.0)
        cube = 0.39 * safe2 * jnp.sqrt(safe2) * lax.rsqrt(both)
        decay = jnp.exp(-cube)
        damp3 = 1.0 - decay
        damp5 = 1.0 - (1.0 + cube) * decay
        ratio = 1.0 - dist2 / (CUTOFF * CUTOFF)
        taper = jnp.where(keep, ratio * ratio, 0.0)
        if dipolar:
            along = jnp.sum(diff * dip[:, None, :], axis=0)
            term = (3.0 * taper * damp5 * inv3 * inverse * inverse * along)[None] * diff - (
                taper * damp3 * inv3
            )[None] * dip[:, None, :]
        else:
            term = (taper * damp3 * inv3 * charge[None, :])[None] * diff
        return (total + jnp.sum(term, axis=2), None)

    start = jnp.zeros((3, target.shape[1]), jnp.float32)
    total, unused = lax.scan(step, start, blocks)
    return total


def body(positions, charges, polar, molecule):
    beads_here = positions.shape[0]
    atoms = positions.shape[2]
    rank = lax.axis_index("bead")
    local = (rank * beads_here + jnp.arange(beads_here, dtype=jnp.int32)).astype(jnp.float32)
    kidx = jnp.arange(CONTR, dtype=jnp.float32)[:, None] / CONTR
    theta = 2.0 * jnp.pi * (kidx - local[None, :] / BEADS)
    series = 1.0 + 2.0 * jnp.cos(theta) + jnp.cos(2.0 * theta)
    contract = series / BEADS
    spread_back = series.T / CONTR
    high = lax.Precision.HIGHEST
    packed = jnp.concatenate(
        [positions.reshape(beads_here * 3, atoms), charges[None], polar[None]], 0
    )
    rim = padded(packed, (("space", 1),), atoms)
    source_pos = rim[: beads_here * 3].reshape(beads_here, 3, 3 * atoms)
    source_charge = rim[beads_here * 3]
    source_alpha = rim[beads_here * 3 + 1]
    outside = jnp.full((atoms,), -1, jnp.int32)
    source_mol = jnp.concatenate([outside, molecule, outside])
    blank_dip = jnp.zeros((3, 3 * atoms), jnp.float32)
    blank_charge = jnp.zeros((3 * atoms,), jnp.float32)
    perm = lax.map(
        lambda pair: pair_field(
            pair[0],
            polar,
            molecule,
            pair[1],
            source_charge,
            source_alpha,
            blank_dip,
            source_mol,
            False,
        ),
        (positions, source_pos),
    )
    stacked = jnp.concatenate([positions, perm], 1)
    contracted = jnp.einsum("kb,bxa->kxa", contract, stacked, precision=high)
    whole = of_everyone(contracted, "bead")
    cpos = whole[:, :3]
    cfield = whole[:, 3:]
    source_cpos = padded(cpos.reshape(CONTR * 3, atoms), (("space", 1),), atoms).reshape(
        CONTR, 3, 3 * atoms
    )

    def induce(dip):
        source_dip = padded(dip.reshape(CONTR * 3, atoms), (("space", 1),), atoms).reshape(
            CONTR, 3, 3 * atoms
        )
        return lax.map(
            lambda item: pair_field(
                item[0],
                polar,
                molecule,
                item[1],
                blank_charge,
                source_alpha,
                item[2],
                source_mol,
                True,
            ),
            (cpos, source_cpos, source_dip),
        )

    moment = polar[None, None, :] * cfield
    for step in range(ITERS):
        moment = polar[None, None, :] * (cfield + induce(moment))
    induced = induce(moment)
    total = perm + jnp.einsum("bk,kxa->bxa", spread_back, induced, precision=high)
    return (total, moment)


def solution(mesh):
    in_specs = (P("bead", None, "space"), P("space"), P("space"), P("space"))
    out_specs = (P("bead", None, "space"), P(None, None, "space"))
    return jax.shard_map(body, mesh=mesh, in_specs=in_specs, out_specs=out_specs, check_vma=False)
```

profile of v0, /device:TPU:217, one launch (start us, length us, event | category | flops | bytes accessed | tf_op | source)
XLA Modules:
  0.0 258.1 jit_solution(17326241371293172586)
XLA Ops:
  14.1 39.8 %while.85 = (s32[]{:T(128)}, f32[4,3,384]{2,0,1:T(4,128)S(1)}, f32[4,3,1152]{2,1,0:T(4,128)S(1)}, f32[1,1152]{1,0:T(1,128)S(1)}, f32[1,1152]{1,0:T(1,128)S(1)}, ...) while((s32[]{:T(128)}, f32[4,3,384]{2,0,1:T(4,128)S(1)}, ...), condition=%wide.region_5.6_spmd, body=%wide.region_0.5_spmd.sunk | while | flops 935109 | bytes 560656 | solution.py:113
  14.5 9.5 %while.92 = (s32[]{:T(128)}, f32[3,384]{1,0:T(4,128)S(1)}, f32[18,64]{1,0:T(8,128)S(1)}, s32[384]{0:T(512)S(1)}, s32[18,64]{1,0:T(8,128)S(1)}, /*index=5*/f32[3,...) while((s32[]{:T(128)}, f32[3,384]{1,0:T(4,128)S(1)}, ...), condition=%wide.region_4.4_spmd.clone, body=%wide.region_1.3_spmd.clone.sunk | while | flops 935107 | bytes 431367 | solution.py:87
  24.5 9.5 %while.92 = (s32[]{:T(128)}, f32[3,384]{1,0:T(4,128)S(1)}, f32[18,64]{1,0:T(8,128)S(1)}, s32[384]{0:T(512)S(1)}, s32[18,64]{1,0:T(8,128)S(1)}, /*index=5*/f32[3,...) while((s32[]{:T(128)}, f32[3,384]{1,0:T(4,128)S(1)}, ...), condition=%wide.region_4.4_spmd.clone, body=%wide.region_1.3_spmd.clone.sunk | while | flops 935107 | bytes 431367 | solution.py:87
  34.4 9.5 %while.92 = (s32[]{:T(128)}, f32[3,384]{1,0:T(4,128)S(1)}, f32[18,64]{1,0:T(8,128)S(1)}, s32[384]{0:T(512)S(1)}, s32[18,64]{1,0:T(8,128)S(1)}, /*index=5*/f32[3,...) while((s32[]{:T(128)}, f32[3,384]{1,0:T(4,128)S(1)}, ...), condition=%wide.region_4.4_spmd.clone, body=%wide.region_1.3_spmd.clone.sunk | while | flops 935107 | bytes 431367 | solution.py:87
  44.4 9.5 %while.92 = (s32[]{:T(128)}, f32[3,384]{1,0:T(4,128)S(1)}, f32[18,64]{1,0:T(8,128)S(1)}, s32[384]{0:T(512)S(1)}, s32[18,64]{1,0:T(8,128)S(1)}, /*index=5*/f32[3,...) while((s32[]{:T(128)}, f32[3,384]{1,0:T(4,128)S(1)}, ...), condition=%wide.region_4.4_spmd.clone, body=%wide.region_1.3_spmd.clone.sunk | while | flops 935107 | bytes 431367 | solution.py:87
  54.3 22.7 %all_to_all.5 = f32[8,4,6,384]{3,1,2,0:T(4,128)S(1)} all-to-all(f32[8,4,6,384]{3,1,2,0:T(4,128)S(1)} %broadcast_in_dim.76), channel_id=1, replica_groups=mesh['bead'=8,'space'=64] {'bead'}, dimensions={0} | all-to-all | bytes 589824 | tf_op jit(solution)/shard_map/all_to_all | solution.py:29
  79.0 7.5 %collective-permute-start.4 = (f32[12,384]{1,0:T(8,128)S(1)}, f32[12,384]{1,0:T(8,128)S(1)}, u32[]{:S(2)}, u32[]{:S(2)}) collective-permute-start(f32[12,384]{1,0:T(8,128)S(1)} %reshape.754), channel_id=1, source_target_pairs={{0,1},{1,2},{2,3},{3,4},{4,5},{5,6},{6,7},{7,8},{8,9},{9,10},{10,1... | collective-permute-start | bytes 55304 | tf_op jit(solution)/shard_map/ppermute | solution.py:19
  97.7 45.8 %while.87 = (s32[]{:T(128)}, f32[4,3,384]{2,0,1:T(4,128)S(1)}, f32[4,3,1152]{2,1,0:T(4,128)S(1)}, f32[1,1152]{1,0:T(1,128)S(1)}, f32[4,3,1152]{2,0,1:T(4,128)S(1...) while((s32[]{:T(128)}, f32[4,3,384]{2,0,1:T(4,128)S(1)}, ...), condition=%wide.region_13.14_spmd, body=%wide.region_7.13_spmd.sunk | while | flops 1402053 | bytes 1022208 | solution.py:140
  98.1 11.0 %while.93 = (s32[]{:T(128)}, f32[3,384]{1,0:T(4,128)S(1)}, f32[18,64]{1,0:T(8,128)S(1)}, s32[384]{0:T(512)S(1)}, s32[18,64]{1,0:T(8,128)S(1)}, /*index=5*/f32[3,...) while((s32[]{:T(128)}, f32[3,384]{1,0:T(4,128)S(1)}, ...), condition=%wide.region_12.12_spmd.clone, body=%wide.region_8.11_spmd.clone.sunk | while | flops 1402051 | bytes 828423 | solution.py:87
  109.6 11.0 %while.93 = (s32[]{:T(128)}, f32[3,384]{1,0:T(4,128)S(1)}, f32[18,64]{1,0:T(8,128)S(1)}, s32[384]{0:T(512)S(1)}, s32[18,64]{1,0:T(8,128)S(1)}, /*index=5*/f32[3,...) while((s32[]{:T(128)}, f32[3,384]{1,0:T(4,128)S(1)}, ...), condition=%wide.region_12.12_spmd.clone, body=%wide.region_8.11_spmd.clone.sunk | while | flops 1402051 | bytes 828423 | solution.py:87
  121.0 11.0 %while.93 = (s32[]{:T(128)}, f32[3,384]{1,0:T(4,128)S(1)}, f32[18,64]{1,0:T(8,128)S(1)}, s32[384]{0:T(512)S(1)}, s32[18,64]{1,0:T(8,128)S(1)}, /*index=5*/f32[3,...) while((s32[]{:T(128)}, f32[3,384]{1,0:T(4,128)S(1)}, ...), condition=%wide.region_12.12_spmd.clone, body=%wide.region_8.11_spmd.clone.sunk | while | flops 1402051 | bytes 828423 | solution.py:87
  132.5 11.0 %while.93 = (s32[]{:T(128)}, f32[3,384]{1,0:T(4,128)S(1)}, f32[18,64]{1,0:T(8,128)S(1)}, s32[384]{0:T(512)S(1)}, s32[18,64]{1,0:T(8,128)S(1)}, /*index=5*/f32[3,...) while((s32[]{:T(128)}, f32[3,384]{1,0:T(4,128)S(1)}, ...), condition=%wide.region_12.12_spmd.clone, body=%wide.region_8.11_spmd.clone.sunk | while | flops 1402051 | bytes 828423 | solution.py:87
  147.9 6.6 %collective-permute-done.7 = f32[12,384]{1,0:T(8,128)S(1)} collective-permute-done((f32[12,384]{1,0:T(8,128)S(1)}, f32[12,384]{1,0:T(8,128)S(1)}, u32[]{:S(2)}, u32[]{:S(2)}) %collective-permute-start.7) | collective-permute-done | bytes 18464 | tf_op jit(solution)/shard_map/ppermute | solution.py:22
  154.6 45.8 %while.89 = (s32[]{:T(128)}, f32[4,3,384]{2,0,1:T(4,128)S(1)}, f32[4,3,1152]{2,1,0:T(4,128)S(1)}, f32[1,1152]{1,0:T(1,128)S(1)}, f32[4,3,1152]{2,0,1:T(4,128)S(1...) while((s32[]{:T(128)}, f32[4,3,384]{2,0,1:T(4,128)S(1)}, ...), condition=%wide.region_20.21_spmd, body=%wide.region_14.20_spmd.sunk | while | flops 1402053 | bytes 1022208 | solution.py:140
  155.0 11.0 %while.94 = (s32[]{:T(128)}, f32[3,384]{1,0:T(4,128)S(1)}, f32[18,64]{1,0:T(8,128)S(1)}, s32[384]{0:T(512)S(1)}, s32[18,64]{1,0:T(8,128)S(1)}, /*index=5*/f32[3,...) while((s32[]{:T(128)}, f32[3,384]{1,0:T(4,128)S(1)}, ...), condition=%wide.region_19.19_spmd.clone, body=%wide.region_15.18_spmd.clone.sunk | while | flops 1402051 | bytes 828423 | solution.py:87
  166.4 11.0 %while.94 = (s32[]{:T(128)}, f32[3,384]{1,0:T(4,128)S(1)}, f32[18,64]{1,0:T(8,128)S(1)}, s32[384]{0:T(512)S(1)}, s32[18,64]{1,0:T(8,128)S(1)}, /*index=5*/f32[3,...) while((s32[]{:T(128)}, f32[3,384]{1,0:T(4,128)S(1)}, ...), condition=%wide.region_19.19_spmd.clone, body=%wide.region_15.18_spmd.clone.sunk | while | flops 1402051 | bytes 828423 | solution.py:87
  177.9 11.0 %while.94 = (s32[]{:T(128)}, f32[3,384]{1,0:T(4,128)S(1)}, f32[18,64]{1,0:T(8,128)S(1)}, s32[384]{0:T(512)S(1)}, s32[18,64]{1,0:T(8,128)S(1)}, /*index=5*/f32[3,...) while((s32[]{:T(128)}, f32[3,384]{1,0:T(4,128)S(1)}, ...), condition=%wide.region_19.19_spmd.clone, body=%wide.region_15.18_spmd.clone.sunk | while | flops 1402051 | bytes 828423 | solution.py:87
  189.3 11.0 %while.94 = (s32[]{:T(128)}, f32[3,384]{1,0:T(4,128)S(1)}, f32[18,64]{1,0:T(8,128)S(1)}, s32[384]{0:T(512)S(1)}, s32[18,64]{1,0:T(8,128)S(1)}, /*index=5*/f32[3,...) while((s32[]{:T(128)}, f32[3,384]{1,0:T(4,128)S(1)}, ...), condition=%wide.region_19.19_spmd.clone, body=%wide.region_15.18_spmd.clone.sunk | while | flops 1402051 | bytes 828423 | solution.py:87
  204.8 6.6 %collective-permute-done.9 = f32[12,384]{1,0:T(8,128)S(1)} collective-permute-done((f32[12,384]{1,0:T(8,128)S(1)}, f32[12,384]{1,0:T(8,128)S(1)}, u32[]{:S(2)}, u32[]{:S(2)}) %collective-permute-start.9) | collective-permute-done | bytes 18464 | tf_op jit(solution)/shard_map/ppermute | solution.py:22
  211.5 45.7 %while.91 = (s32[]{:T(128)}, f32[4,3,384]{2,0,1:T(4,128)S(1)}, f32[4,3,1152]{2,1,0:T(4,128)S(1)}, f32[1,1152]{1,0:T(1,128)S(1)}, f32[4,3,1152]{2,0,1:T(4,128)S(1...) while((s32[]{:T(128)}, f32[4,3,384]{2,0,1:T(4,128)S(1)}, ...), condition=%wide.region_27.28_spmd, body=%wide.region_21.27_spmd.sunk | while | flops 1402053 | bytes 1022208 | solution.py:140
  211.9 10.9 %while.95 = (s32[]{:T(128)}, f32[3,384]{1,0:T(4,128)S(1)}, f32[18,64]{1,0:T(8,128)S(1)}, s32[384]{0:T(512)S(1)}, s32[18,64]{1,0:T(8,128)S(1)}, /*index=5*/f32[3,...) while((s32[]{:T(128)}, f32[3,384]{1,0:T(4,128)S(1)}, ...), condition=%wide.region_26.26_spmd.clone, body=%wide.region_22.25_spmd.clone.sunk | while | flops 1402051 | bytes 828423 | solution.py:87
  223.3 10.9 %while.95 = (s32[]{:T(128)}, f32[3,384]{1,0:T(4,128)S(1)}, f32[18,64]{1,0:T(8,128)S(1)}, s32[384]{0:T(512)S(1)}, s32[18,64]{1,0:T(8,128)S(1)}, /*index=5*/f32[3,...) while((s32[]{:T(128)}, f32[3,384]{1,0:T(4,128)S(1)}, ...), condition=%wide.region_26.26_spmd.clone, body=%wide.region_22.25_spmd.clone.sunk | while | flops 1402051 | bytes 828423 | solution.py:87
  234.7 10.9 %while.95 = (s32[]{:T(128)}, f32[3,384]{1,0:T(4,128)S(1)}, f32[18,64]{1,0:T(8,128)S(1)}, s32[384]{0:T(512)S(1)}, s32[18,64]{1,0:T(8,128)S(1)}, /*index=5*/f32[3,...) while((s32[]{:T(128)}, f32[3,384]{1,0:T(4,128)S(1)}, ...), condition=%wide.region_26.26_spmd.clone, body=%wide.region_22.25_spmd.clone.sunk | while | flops 1402051 | bytes 828423 | solution.py:87
  246.2 10.9 %while.95 = (s32[]{:T(128)}, f32[3,384]{1,0:T(4,128)S(1)}, f32[18,64]{1,0:T(8,128)S(1)}, s32[384]{0:T(512)S(1)}, s32[18,64]{1,0:T(8,128)S(1)}, /*index=5*/f32[3,...) while((s32[]{:T(128)}, f32[3,384]{1,0:T(4,128)S(1)}, ...), condition=%wide.region_26.26_spmd.clone, body=%wide.region_22.25_spmd.clone.sunk | while | flops 1402051 | bytes 828423 | solution.py:87
  (3074 shorter events, 189.1 us)
Async XLA Ops:
  1.4 0.7 copy-start.4
  2.0 0.7 copy-start
  2.7 5.2 %collective-permute-start = (f32[14,384]{1,0:T(8,128)S(1)}, f32[14,384]{1,0:T(8,128)S(1)}, u32[]{:S(2)}, u32[]{:S(2)}) collective-permute-start(f32[14,384]{1,0:T(8,128)S(1)} %pad_maximum_fusion.5), channel_id=1, source_target_pairs={{0,1},{1,2},{2,3},{3,4},{4,5},{5,6},{6,7},{7,8},{8,9},{9,10},{10,1... | collective-permute-start | bytes 64520 | tf_op jit(solution)/shard_map/ppermute | solution.py:19
  5.0 9.1 %collective-permute-start.1 = (f32[14,384]{1,0:T(8,128)S(1)}, f32[14,384]{1,0:T(8,128)S(1)}, u32[]{:S(2)}, u32[]{:S(2)}) collective-permute-start(f32[14,384]{1,0:T(8,128)S(1)} %pad_maximum_fusion.5), channel_id=1, source_target_pairs={{1,0},{2,1},{3,2},{4,3},{5,4},{6,5},{7,6},{8,7},{9,8},{10,9},{11,1... | collective-permute-start | bytes 64520 | tf_op jit(solution)/shard_map/ppermute | solution.py:22
  7.3 0.7 copy-start.1
  14.1 39.8 %copy-start.3 = (f32[4,3,384]{2,0,1:T(4,128)S(1)}, f32[4,3,384]{2,0,1:T(4,128)}, u32[]{:S(2)}) copy-start(f32[4,3,384]{2,0,1:T(4,128)} %param.20) | copy-start | bytes 55300
  77.1 13.9 %collective-permute-start.5 = (f32[12,384]{1,0:T(8,128)S(1)}, f32[12,384]{1,0:T(8,128)S(1)}, u32[]{:S(2)}, u32[]{:S(2)}) collective-permute-start(f32[12,384]{1,0:T(8,128)S(1)} %reshape.754), channel_id=1, source_target_pairs={{1,0},{2,1},{3,2},{4,3},{5,4},{6,5},{7,6},{8,7},{9,8},{10,9},{11,1... | collective-permute-start | bytes 55304 | tf_op jit(solution)/shard_map/ppermute | solution.py:22
  79.0 12.0 %collective-permute-start.4 = (f32[12,384]{1,0:T(8,128)S(1)}, f32[12,384]{1,0:T(8,128)S(1)}, u32[]{:S(2)}, u32[]{:S(2)}) collective-permute-start(f32[12,384]{1,0:T(8,128)S(1)} %reshape.754), channel_id=1, source_target_pairs={{0,1},{1,2},{2,3},{3,4},{4,5},{5,6},{6,7},{7,8},{8,9},{9,10},{10,1... | collective-permute-start | bytes 55304 | tf_op jit(solution)/shard_map/ppermute | solution.py:19
  86.6 4.4 %collective-permute-start.2 = (f32[12,384]{1,0:T(8,128)S(1)}, f32[12,384]{1,0:T(8,128)S(1)}, u32[]{:S(2)}, u32[]{:S(2)}) collective-permute-start(f32[12,384]{1,0:T(8,128)S(1)} %reshape.753), channel_id=1, source_target_pairs={{0,1},{1,2},{2,3},{3,4},{4,5},{5,6},{6,7},{7,8},{8,9},{9,10},{10,1... | collective-permute-start | bytes 55304 | tf_op jit(solution)/shard_map/ppermute | solution.py:19
  88.6 9.1 %collective-permute-start.3 = (f32[12,384]{1,0:T(8,128)S(1)}, f32[12,384]{1,0:T(8,128)S(1)}, u32[]{:S(2)}, u32[]{:S(2)}) collective-permute-start(f32[12,384]{1,0:T(8,128)S(1)} %reshape.753), channel_id=1, source_target_pairs={{1,0},{2,1},{3,2},{4,3},{5,4},{6,5},{7,6},{8,7},{9,8},{10,9},{11,1... | collective-permute-start | bytes 55304 | tf_op jit(solution)/shard_map/ppermute | solution.py:22
  143.6 4.3 %collective-permute-start.6 = (f32[12,384]{1,0:T(8,128)S(1)}, f32[12,384]{1,0:T(8,128)S(1)}, u32[]{:S(2)}, u32[]{:S(2)}) collective-permute-start(f32[12,384]{1,0:T(8,128)S(1)} %reshape.755), channel_id=1, source_target_pairs={{0,1},{1,2},{2,3},{3,4},{4,5},{5,6},{6,7},{7,8},{8,9},{9,10},{10,1... | collective-permute-start | bytes 55304 | tf_op jit(solution)/shard_map/ppermute | solution.py:19
  145.5 9.1 %collective-permute-start.7 = (f32[12,384]{1,0:T(8,128)S(1)}, f32[12,384]{1,0:T(8,128)S(1)}, u32[]{:S(2)}, u32[]{:S(2)}) collective-permute-start(f32[12,384]{1,0:T(8,128)S(1)} %reshape.755), channel_id=1, source_target_pairs={{1,0},{2,1},{3,2},{4,3},{5,4},{6,5},{7,6},{8,7},{9,8},{10,9},{11,1... | collective-permute-start | bytes 55304 | tf_op jit(solution)/shard_map/ppermute | solution.py:22
  200.4 11.1 %copy-start.2 = (f32[4,3,384]{2,0,1:T(4,128)}, f32[4,3,384]{2,0,1:T(4,128)S(1)}, u32[]{:S(2)}) copy-start(f32[4,3,384]{2,0,1:T(4,128)S(1)} %add_multiply_fusion) | copy-start | bytes 55300
  200.4 4.3 %collective-permute-start.8 = (f32[12,384]{1,0:T(8,128)S(1)}, f32[12,384]{1,0:T(8,128)S(1)}, u32[]{:S(2)}, u32[]{:S(2)}) collective-permute-start(f32[12,384]{1,0:T(8,128)S(1)} %reshape.756), channel_id=1, source_target_pairs={{0,1},{1,2},{2,3},{3,4},{4,5},{5,6},{6,7},{7,8},{8,9},{9,10},{10,1... | collective-permute-start | bytes 55304 | tf_op jit(solution)/shard_map/ppermute | solution.py:19
  202.4 9.1 %collective-permute-start.9 = (f32[12,384]{1,0:T(8,128)S(1)}, f32[12,384]{1,0:T(8,128)S(1)}, u32[]{:S(2)}, u32[]{:S(2)}) collective-permute-start(f32[12,384]{1,0:T(8,128)S(1)} %reshape.756), channel_id=1, source_target_pairs={{1,0},{2,1},{3,2},{4,3},{5,4},{6,5},{7,6},{8,7},{9,8},{10,9},{11,1... | collective-permute-start | bytes 55304 | tf_op jit(solution)/shard_map/ppermute | solution.py:22
where the time goes:
time: 259 us; the launch traced here: 258 us
  other arithmetic  135 us (52%)
  starting transfers between devices  27 us (10%)
  waiting for transfers between devices  25.8 us (10%)
  loops' own time  24.5 us (9%)
  blocking collectives  22.7 us (9%)
  local copies, waits for them, and re-layouts  20.9 us (8%)
    mul x216, other arithmetic, step(): 3.0 * taper * damp5 * inv3 * inverse * inverse * along  42.9 us
    reduce_sum x288, other arithmetic, step(): return (total + jnp.sum(term, axis=2), None)  38.3 us
    ppermute x5, waiting for transfers between devices, padded(): lax.ppermute(lax.slice_in_dim(block, 0, width, axis=dim), axis, backward)  25.8 us
    reduce_sum x216, other arithmetic, step(): along = jnp.sum(diff * dip[:, None, :], axis=0)  25.6 us
    another operation x16, loops' own time, pair_field(): total, unused = lax.scan(step, start, blocks)  23.5 us
    all_to_all x1, blocking collectives, copy_for_each(): return lax.all_to_all(copies, axis, split_axis=0, concat_axis=0, tiled=True)  22.7 us
    ppermute x5, starting transfers between devices, padded(): lax.ppermute(lax.slice_in_dim(block, block.shape[dim] - width, None, axis...  15.6 us
    mul x72, other arithmetic, step(): term = (taper * damp3 * inv3 * charge[None, :])[None] * diff  12.5 us
  transfers between devices with their start and end apart: 10, of which 4 were waited for; matrix products, arithmetic and copies ran while one was open for 0% of the time, Pallas kernels for 0%

commit v1 on v0

v1 whole, which is shorter than its diff:
```python
import functools
import math

import jax
import jax.numpy as jnp
import numpy as np
from jax import lax
from jax.experimental import pallas as pl
from jax.experimental.pallas import tpu as pltpu
from jax.sharding import PartitionSpec as P

BEADS = 32
CONTR = 4
ITERS = 2
CUT2 = 81.0
MESH = pl.DeviceIdType.MESH
OWN, LEFT, RIGHT = 0, 1, 2


def series(i):
    theta = 2.0 * math.pi * i / BEADS
    return (1.0 + 2.0 * math.cos(theta) + math.cos(2.0 * theta)) / BEADS


def kernel(
    beads, atoms, spaces,
    pos_hbm, charge_hbm, polar_hbm, mol_hbm,
    total_ref, moment_ref,
    pos_ref, charge_ref, polar_ref, mol_ref, in_sem,
    pk, col, perm, cps, cpin, fps, fpin, ctr, ccol, tens, mu, mucol, ind, indin, muin,
    halo_send, halo_recv, cp_send, cp_recv, fp_send, fp_recv, mu_send, mu_recv,
    dip_send, dip_recv, ind_send, ind_recv,
):
    rank = lax.axis_index("bead")
    slab = lax.axis_index("space")
    half, spot = rank // 4, lax.rem(rank, 4)
    left, right = lax.rem(slab + spaces - 1, spaces), lax.rem(slab + 1, spaces)
    row_first, row_last = lax.rem(slab, 8) == 0, lax.rem(slab, 8) == 7
    across = (1 - half) * 4 + spot
    to_left = (rank, left)
    to_right = (rank, right)
    mu_left = (jnp.where(row_first, across, rank), left)
    mu_right = (jnp.where(row_last, across, rank), right)

    slabs = (slab, left, right)

    def peer(turn, dx, side=OWN):
        return ((half if turn == 0 else 1 - half) * 4 + lax.rem(spot + dx, 4), slabs[side])

    others = [(turn, dx) for turn in (1, 0) for dx in (2, 1, 3, 0) if (turn, dx) != (0, 0)]
    around = [(turn, dx, side) for turn in (1, 0) for dx in (2, 1, 3, 0) for side in (LEFT, RIGHT, OWN)]
    around.remove((0, 0, OWN))
    barrier = pltpu.get_barrier_semaphore()
    greeted = [peer(*o) for o in around]
    for device in greeted:
        pl.semaphore_signal(barrier, inc=1, device_id=device, device_id_type=MESH)

    loads = [
        pltpu.make_async_copy(src, dst, in_sem.at[n])
        for n, (src, dst) in enumerate(
            ((pos_hbm, pos_ref), (charge_hbm, charge_ref), (polar_hbm, polar_ref), (mol_hbm, mol_ref))
        )
    ]
    for c in loads:
        c.start()

    def remote(src, dst, send, recv, device):
        return pltpu.make_async_remote_copy(
            src_ref=src, dst_ref=dst, send_sem=send, recv_sem=recv, device_id=device, device_id_type=MESH
        )

    def weight(k, l):
        j = lax.rem(2 * k - rank + 8, 8)
        value = jnp.float32(series(-l))
        for n in range(1, 8):
            value = jnp.where(j == n, jnp.float32(series(4 * n - l)), value)
        return value

    fold = [[weight(lax.rem(spot + dx, 4), l) for l in range(beads)] for dx in range(4)]
    for c in loads:
        c.wait()
    for a in range(3):
        pk[OWN, 4 * a : 4 * a + 4, :] = pos_ref[a]
    alpha = polar_ref[...].reshape(1, atoms)
    root = lax.rsqrt(alpha) * math.sqrt(0.39)
    pk[OWN, 12:13, :] = charge_ref[...].reshape(1, atoms) * (1.0 / (CUT2 * CUT2))
    pk[OWN, 13:14, :] = -root
    pk[OWN, 14:15, :] = mol_ref[...].astype(jnp.float32).reshape(1, atoms)
    pk[OWN, 15:16, :] = alpha

    pl.semaphore_wait(barrier, len(greeted))
    halo = [
        remote(pk.at[OWN], pk.at[RIGHT], halo_send.at[0], halo_recv.at[0], to_left),
        remote(pk.at[OWN], pk.at[LEFT], halo_send.at[1], halo_recv.at[1], to_right),
    ]
    for c in halo:
        c.start()

    def spread(row):
        return jnp.broadcast_to(row, (8, atoms))

    col[OWN] = pk[OWN].T
    gi = spread(root)
    moli = spread(pk[OWN, 14:15, :])
    zero = jnp.zeros((8, atoms), jnp.float32)

    def perm_part(l, side, start):
        target = [spread(pk[OWN, 4 * a + l : 4 * a + l + 1, :]) for a in range(3)]

        def step(i, acc):
            source = col[side, pl.ds(i * 8, 8), :]
            d = [target[a] - source[:, 4 * a + l : 4 * a + l + 1] for a in range(3)]
            r2 = d[0] * d[0] + d[1] * d[1] + d[2] * d[2]
            if side == OWN:
                r2 = jnp.where(moli == source[:, 14:15], CUT2, r2)
            r2 = jnp.minimum(r2, CUT2)
            inv = lax.rsqrt(r2)
            c = (r2 * gi) * source[:, 13:14] * (r2 * inv)
            decay = jnp.exp(c)
            u = (CUT2 - r2) * inv
            w = (u * u) * (inv * source[:, 12:13]) * (1.0 - decay)
            return tuple(acc[a] + w * d[a] for a in range(3))

        return lax.fori_loop(0, atoms // 8, step, start, unroll=atoms // 8)

    fields = [perm_part(l, OWN, (zero, zero, zero)) for l in range(beads)]
    for l in range(beads):
        for a in range(3):
            perm[l, a] = fields[l][a]

    for c in halo:
        c.wait_recv()
    for side in (LEFT, RIGHT):
        col[side] = pk[side].T

    for side in (OWN, LEFT, RIGHT):
        for a in range(3):
            spots = [pk[side, 4 * a + l : 4 * a + l + 1, :] for l in range(beads)]
            for dx in range(4):
                cps[dx, side, a : a + 1, :] = sum(fold[dx][l] * spots[l] for l in range(beads))
    sends = []
    for n, (turn, dx) in enumerate(others):
        sends.append(remote(cps.at[dx], cpin.at[n], cp_send.at[n], cp_recv.at[n], peer(turn, dx)))
        sends[-1].start()
    cp_copies = list(sends)

    for l in range(beads):
        acc = tuple(perm[l, a] for a in range(3))
        acc = perm_part(l, LEFT, acc)
        acc = perm_part(l, RIGHT, acc)
        for a in range(3):
            perm[l, a] = acc[a]
    rows = [
        jnp.concatenate([jnp.sum(perm[l, a], axis=0, keepdims=True) for a in range(3)], 0) for l in range(beads)
    ]
    for dx in range(4):
        fps[dx] = sum(fold[dx][l] * rows[l] for l in range(beads))
    fp_copies = []
    facing = {OWN: OWN, LEFT: RIGHT, RIGHT: LEFT}
    for turn, dx, side in around:
        n = (facing[side], turn * 4 + dx)
        fp_copies.append(remote(fps.at[dx], fpin.at[n], fp_send.at[n], fp_recv.at[n], peer(turn, dx, side)))
        fp_copies[-1].start()

    for c in cp_copies:
        c.wait_recv()
    for side in (OWN, LEFT, RIGHT):
        whole = cps[0, side]
        for n in range(len(others)):
            whole = whole + cpin[n, side]
        ctr[side, 0:3, :] = whole
        ctr[side, 3:8, :] = jnp.zeros((5, atoms), jnp.float32)
        ccol[side] = ctr[side].T

    target = [spread(ctr[OWN, a : a + 1, :]) for a in range(3)]
    for side in (OWN, LEFT, RIGHT):

        def step(i, carry, side=side):
            at = pl.ds(i * 8, 8)
            source = col[side, at, :]
            where = ccol[side, at, :]
            d = [target[a] - where[:, a : a + 1] for a in range(3)]
            r2 = d[0] * d[0] + d[1] * d[1] + d[2] * d[2]
            if side == OWN:
                r2 = jnp.where(moli == source[:, 14:15], CUT2, r2)
            r2 = jnp.minimum(r2, CUT2)
            inv = lax.rsqrt(r2)
            c = (r2 * gi) * source[:, 13:14] * (r2 * inv)
            decay = jnp.exp(c)
            damp3 = 1.0 - decay
            damp5 = damp3 + c * decay
            u = (CUT2 - r2) * (inv * (1.0 / CUT2))
            v = u * u * inv
            w3 = v * damp3
            w5 = (3.0 * v) * (inv * inv) * damp5
            e = [w5 * d[a] for a in range(3)]
            tens[side, 0, at, :] = e[0] * d[0] - w3
            tens[side, 1, at, :] = e[1] * d[1] - w3
            tens[side, 2, at, :] = e[2] * d[2] - w3
            tens[side, 3, at, :] = e[0] * d[1]
            tens[side, 4, at, :] = e[0] * d[2]
            tens[side, 5, at, :] = e[1] * d[2]
            return carry

        lax.fori_loop(0, atoms // 8, step, 0, unroll=atoms // 8)

    for c in fp_copies:
        c.wait_recv()
    fpin[OWN, 0] = fps[0]
    fields = [sum(fpin[side, n] for n in range(8)) for side in (OWN, LEFT, RIGHT)]
    cfield = fields[OWN]

    def induce_part(step_no, side, acc):
        def step(i, acc):
            at = pl.ds(i * 8, 8)
            m = mucol[side, at, :]
            m = [m[:, a : a + 1] for a in range(3)]
            t = [tens[side, n, at, :] for n in range(6)]
            return (
                acc[0] + (t[0] * m[0] + t[3] * m[1] + t[4] * m[2]),
                acc[1] + (t[3] * m[0] + t[1] * m[1] + t[5] * m[2]),
                acc[2] + (t[4] * m[0] + t[5] * m[1] + t[2] * m[2]),
            )

        return lax.fori_loop(0, atoms // 8, step, acc, unroll=atoms // 8)

    mu_copies = []
    dip_copies = []

    def columns(moment, side):
        wide = jnp.concatenate([moment, jnp.zeros((5, atoms), jnp.float32)], 0)
        mucol[side] = wide.T

    def rows_of(acc):
        return jnp.concatenate([jnp.sum(acc[a], axis=0, keepdims=True) for a in range(3)], 0)

    def induce_first():
        acc = (zero, zero, zero)
        for side in (OWN, LEFT, RIGHT):
            columns(pk[side, 15:16, :] * fields[side], side)
            acc = induce_part(0, side, acc)
        return rows_of(acc)

    def induce(n, moment):
        mu[n, OWN] = moment
        copies = [
            remote(mu.at[n, OWN], mu.at[n, RIGHT], mu_send.at[n, 0], mu_recv.at[n, 0], mu_left),
            remote(mu.at[n, OWN], mu.at[n, LEFT], mu_send.at[n, 1], mu_recv.at[n, 1], mu_right),
        ]
        for c in copies:
            c.start()
        mu_copies.extend(copies)
        if n == ITERS:
            for dx in (2, 1, 3):
                c = remote(mu.at[n, OWN], muin.at[dx], dip_send.at[dx], dip_recv.at[dx], peer(0, dx))
                c.start()
                dip_copies.append(c)

        columns(moment, OWN)
        acc = induce_part(n, OWN, (zero, zero, zero))
        for c, side in zip(copies, (RIGHT, LEFT)):
            c.wait_recv()
            columns(mu[n, side], side)
            acc = induce_part(n, side, acc)
        return rows_of(acc)

    moment = alpha * (cfield + induce_first())
    for n in range(1, ITERS):
        moment = alpha * (cfield + induce(n, moment))
    ind[...] = induce(ITERS, moment)
    ind_copies = []
    for dx in (2, 1, 3):
        c = remote(ind, indin.at[dx], ind_send.at[dx], ind_recv.at[dx], peer(0, dx))
        c.start()
        ind_copies.append(c)

    def put_moment(k, value):
        for a in range(3):
            moment_ref[a, pl.ds(k, 1), :] = value[a : a + 1]

    put_moment(spot, moment)
    total = [rows[l] + (8.0 * fold[0][l]) * ind[...] for l in range(beads)]
    for c, dx in zip(dip_copies, (2, 1, 3)):
        c.wait_recv()
        put_moment(lax.rem(spot + 4 - dx, 4), muin[dx])
    for c, dx in zip(ind_copies, (2, 1, 3)):
        c.wait_recv()
        total = [total[l] + (8.0 * fold[4 - dx][l]) * indin[dx] for l in range(beads)]
    for l in range(beads):
        for a in range(3):
            total_ref[a, l : l + 1, :] = total[l][a : a + 1]
    for c in halo + cp_copies + fp_copies + mu_copies + dip_copies + ind_copies:
        c.wait_send()


def solution(mesh):
    spaces = mesh.shape["space"]

    def body(positions, charges, polar, molecule):
        beads, _, atoms = positions.shape
        f32 = jnp.float32
        vmem = pl.BlockSpec(memory_space=pltpu.VMEM)
        dma = pltpu.SemaphoreType.DMA
        rounds = ITERS + 1
        total, moment = pl.pallas_call(
            functools.partial(kernel, beads, atoms, spaces),
            out_shape=(
                jax.ShapeDtypeStruct((3, beads, atoms), f32),
                jax.ShapeDtypeStruct((3, CONTR, atoms), f32),
            ),
            in_specs=[pl.BlockSpec(memory_space=pltpu.HBM)] * 4,
            out_specs=(vmem, vmem),
            scratch_shapes=[
                pltpu.VMEM((3, beads, atoms), f32),
                pltpu.VMEM((atoms,), f32), pltpu.VMEM((atoms,), f32), pltpu.VMEM((atoms,), jnp.int32),
                dma((4,)),
                pltpu.VMEM((3, 16, atoms), f32),
                pltpu.VMEM((3, atoms, 16), f32),
                pltpu.VMEM((beads, 3, 8, atoms), f32),
                pltpu.VMEM((4, 3, 3, atoms), f32),
                pltpu.VMEM((7, 3, 3, atoms), f32),
                pltpu.VMEM((4, 3, atoms), f32),
                pltpu.VMEM((3, 8, 3, atoms), f32),
                pltpu.VMEM((3, 8, atoms), f32),
                pltpu.VMEM((3, atoms, 8), f32),
                pltpu.VMEM((3, 6, atoms, atoms), f32),
                pltpu.VMEM((rounds, 3, 3, atoms), f32),
                pltpu.VMEM((3, atoms, 8), f32),
                pltpu.VMEM((3, atoms), f32),
                pltpu.VMEM((4, 3, atoms), f32),
                pltpu.VMEM((4, 3, atoms), f32),
                dma((2,)), dma((2,)),
                dma((7,)), dma((7,)),
                dma((3, 8)), dma((3, 8)),
                dma((rounds, 2)), dma((rounds, 2)),
                dma((4,)), dma((4,)),
                dma((4,)), dma((4,)),
            ],
            compiler_params=pltpu.CompilerParams(
                collective_id=0, has_side_effects=True, vmem_limit_bytes=60 * 1024 * 1024
            ),
            name="polarize",
        )(
            positions.transpose(1, 0, 2), charges, polar, molecule
        )
        return total.transpose(1, 0, 2), moment.transpose(1, 0, 2)

    in_specs = (P("bead", None, "space"), P("space"), P("space"), P("space"))
    out_specs = (P("bead", None, "space"), P(None, None, "space"))
    return jax.shard_map(body, mesh=mesh, in_specs=in_specs, out_specs=out_specs, check_vma=False)
```

time: 259 us -> 48.3 us (0.19)
  the two profiles are of different devices: /device:TPU:217 before, /device:TPU:2 now
where the time goes in v1:
time: 48.3 us; the launch traced here: 48 us
  Pallas kernels  45.4 us (94%)
  local copies, waits for them, and re-layouts  1.95 us (4%)
  between operations  0.65 us (1%)
    pallas_call x1, Pallas kernels, body(): pl.pallas_call(functools.partial(kernel, beads, atoms, spaces), out_shape...  45.4 us
    unnamed x4, local copies, waits for them, and re-layouts  1.95 us

profile of v1, /device:TPU:2, one launch (start us, length us, event | category | flops | bytes accessed | tf_op | source)
XLA Modules:
  0.0 48.0 jit_solution(2461858518852493726)
XLA Ops:
  0.6 45.4 %polarize.1 = (f32[3,4,384]{2,1,0:T(4,128)}, f32[3,4,384]{2,1,0:T(4,128)}) custom-call(f32[3,4,384]{2,1,0:T(4,128)} %bitcast.3, f32[384]{0:T(512)} %charge_hbm.1, f32[384]{0:T(512)} %polar_hbm.1, s32[384]{0:T(512)} %mol_hbm.1), custom_call_target="tpu_custom_call" | custom-call | tf_op jit(solution)/shard_map/polarize/pallas_call | solution.py:305
  46.1 0.0 copy-start
  46.1 1.3 %copy.8 = f32[4,3,384]{2,0,1:T(4,128)} copy(f32[4,3,384]{2,0,1:T(4,128)} %bitcast.5) | data formatting | bytes 36864
  47.4 0.0 copy-done
  47.4 0.6 %copy.9 = f32[4,3,384]{2,0,1:T(4,128)} copy(f32[4,3,384]{2,0,1:T(4,128)S(1)} %bitcast.4) | data formatting | bytes 36864
Async XLA Ops:
  46.1 1.3 %copy-start = (f32[3,4,384]{2,1,0:T(4,128)S(1)}, f32[3,4,384]{2,1,0:T(4,128)}, u32[]{:S(2)}) copy-start(f32[3,4,384]{2,1,0:T(4,128)} %get-tuple-element.5) | copy-start | bytes 55300

commit v2 on v1

--- a/solution.py
+++ b/solution.py
@@ -14,7 +14,7 @@
 ITERS = 2
 CUT2 = 81.0
 MESH = pl.DeviceIdType.MESH
-OWN, LEFT, RIGHT = 0, 1, 2
+OWN, NEAR, FAR = 0, 1, 2
 
 
 def series(i):
@@ -26,7 +26,7 @@
     beads, atoms, spaces,
     pos_hbm, charge_hbm, polar_hbm, mol_hbm,
     total_ref, moment_ref,
-    pos_ref, charge_ref, polar_ref, mol_ref, in_sem,
+    pos_ref, charge_ref, polar_ref, mol_ref, in_sem, ready,
     pk, col, perm, cps, cpin, fps, fpin, ctr, ccol, tens, mu, mucol, ind, indin, muin,
     halo_send, halo_recv, cp_send, cp_recv, fp_send, fp_recv, mu_send, mu_recv,
     dip_send, dip_recv, ind_send, ind_recv,
@@ -34,24 +34,25 @@
     rank = lax.axis_index("bead")
     slab = lax.axis_index("space")
     half, spot = rank // 4, lax.rem(rank, 4)
-    left, right = lax.rem(slab + spaces - 1, spaces), lax.rem(slab + 1, spaces)
-    row_first, row_last = lax.rem(slab, 8) == 0, lax.rem(slab, 8) == 7
+    way = 1 - 2 * lax.rem(slab, 2)
+    near, far = slab + way, lax.rem(slab - way + spaces, spaces)
+    row_end = (lax.rem(slab, 8) == 0) | (lax.rem(slab, 8) == 7)
     across = (1 - half) * 4 + spot
-    to_left = (rank, left)
-    to_right = (rank, right)
-    mu_left = (jnp.where(row_first, across, rank), left)
-    mu_right = (jnp.where(row_last, across, rank), right)
-
-    slabs = (slab, left, right)
+    to_near = (rank, near)
+    to_far = (rank, far)
+    mu_far = (jnp.where(row_end, across, rank), far)
+    slabs = (slab, near, far)
 
     def peer(turn, dx, side=OWN):
         return ((half if turn == 0 else 1 - half) * 4 + lax.rem(spot + dx, 4), slabs[side])
 
     others = [(turn, dx) for turn in (1, 0) for dx in (2, 1, 3, 0) if (turn, dx) != (0, 0)]
-    around = [(turn, dx, side) for turn in (1, 0) for dx in (2, 1, 3, 0) for side in (LEFT, RIGHT, OWN)]
+    around = [(turn, dx, side) for turn in (1, 0) for dx in (2, 1, 3, 0) for side in (FAR, NEAR, OWN)]
     around.remove((0, 0, OWN))
     barrier = pltpu.get_barrier_semaphore()
-    greeted = [peer(*o) for o in around]
+    greeted = [peer(1, 0), peer(1, 0, NEAR), peer(1, 0, FAR), to_near, to_far]
+    row = [peer(0, dx) for dx in (2, 1, 3)]
+    greeted += row
     for device in greeted:
         pl.semaphore_signal(barrier, inc=1, device_id=device, device_id_type=MESH)
 
@@ -90,11 +91,13 @@
 
     pl.semaphore_wait(barrier, len(greeted))
     halo = [
-        remote(pk.at[OWN], pk.at[RIGHT], halo_send.at[0], halo_recv.at[0], to_left),
-        remote(pk.at[OWN], pk.at[LEFT], halo_send.at[1], halo_recv.at[1], to_right),
+        remote(pk.at[OWN], pk.at[NEAR], halo_send.at[0], halo_recv.at[0], to_near),
+        remote(pk.at[OWN], pk.at[FAR], halo_send.at[1], halo_recv.at[1], to_far),
     ]
-    for c in halo:
+    for c in halo[::-1]:
         c.start()
+    for device in row:
+        pl.semaphore_signal(ready, inc=1, device_id=device, device_id_type=MESH)
 
     def spread(row):
         return jnp.broadcast_to(row, (8, atoms))
@@ -128,43 +131,44 @@
         for a in range(3):
             perm[l, a] = fields[l][a]
 
-    for c in halo:
-        c.wait_recv()
-    for side in (LEFT, RIGHT):
+    def perm_from(side):
+        if side == NEAR:
+            halo[0].wait_recv()
         col[side] = pk[side].T
-
-    for side in (OWN, LEFT, RIGHT):
+        for l in range(beads):
+            acc = perm_part(l, side, tuple(perm[l, a] for a in range(3)))
+            for a in range(3):
+                perm[l, a] = acc[a]
+
+    perm_from(NEAR)
+    halo[1].wait_recv()
+    for side in (OWN, NEAR, FAR):
         for a in range(3):
             spots = [pk[side, 4 * a + l : 4 * a + l + 1, :] for l in range(beads)]
             for dx in range(4):
                 cps[dx, side, a : a + 1, :] = sum(fold[dx][l] * spots[l] for l in range(beads))
+    pl.semaphore_wait(ready, len(row))
     sends = []
     for n, (turn, dx) in enumerate(others):
         sends.append(remote(cps.at[dx], cpin.at[n], cp_send.at[n], cp_recv.at[n], peer(turn, dx)))
         sends[-1].start()
     cp_copies = list(sends)
 
-    for l in range(beads):
-        acc = tuple(perm[l, a] for a in range(3))
-        acc = perm_part(l, LEFT, acc)
-        acc = perm_part(l, RIGHT, acc)
-        for a in range(3):
-            perm[l, a] = acc[a]
+    perm_from(FAR)
     rows = [
         jnp.concatenate([jnp.sum(perm[l, a], axis=0, keepdims=True) for a in range(3)], 0) for l in range(beads)
     ]
     for dx in range(4):
         fps[dx] = sum(fold[dx][l] * rows[l] for l in range(beads))
     fp_copies = []
-    facing = {OWN: OWN, LEFT: RIGHT, RIGHT: LEFT}
     for turn, dx, side in around:
-        n = (facing[side], turn * 4 + dx)
+        n = (side, turn * 4 + dx)
         fp_copies.append(remote(fps.at[dx], fpin.at[n], fp_send.at[n], fp_recv.at[n], peer(turn, dx, side)))
         fp_copies[-1].start()
 
     for c in cp_copies:
         c.wait_recv()
-    for side in (OWN, LEFT, RIGHT):
+    for side in (OWN, NEAR, FAR):
         whole = cps[0, side]
         for n in range(len(others)):
             whole = whole + cpin[n, side]
@@ -173,7 +177,7 @@
         ccol[side] = ctr[side].T
 
     target = [spread(ctr[OWN, a : a + 1, :]) for a in range(3)]
-    for side in (OWN, LEFT, RIGHT):
+    for side in (OWN, NEAR, FAR):
 
         def step(i, carry, side=side):
             at = pl.ds(i * 8, 8)
@@ -189,17 +193,12 @@
             decay = jnp.exp(c)
             damp3 = 1.0 - decay
             damp5 = damp3 + c * decay
-            u = (CUT2 - r2) * (inv * (1.0 / CUT2))
-            v = u * u * inv
-            w3 = v * damp3
-            w5 = (3.0 * v) * (inv * inv) * damp5
-            e = [w5 * d[a] for a in range(3)]
-            tens[side, 0, at, :] = e[0] * d[0] - w3
-            tens[side, 1, at, :] = e[1] * d[1] - w3
-            tens[side, 2, at, :] = e[2] * d[2] - w3
-            tens[side, 3, at, :] = e[0] * d[1]
-            tens[side, 4, at, :] = e[0] * d[2]
-            tens[side, 5, at, :] = e[1] * d[2]
+            u = (CUT2 - r2) * inv
+            lift = jnp.maximum(inv * damp5, 1e-30)
+            stretch = (u * inv) * (lift * lax.rsqrt(lift))
+            for a in range(3):
+                tens[side, a, at, :] = stretch * d[a]
+            tens[side, 3, at, :] = (u * u) * inv * (damp3 * (1.0 / 3.0))
             return carry
 
         lax.fori_loop(0, atoms // 8, step, 0, unroll=atoms // 8)
@@ -207,7 +206,7 @@
     for c in fp_copies:
         c.wait_recv()
     fpin[OWN, 0] = fps[0]
-    fields = [sum(fpin[side, n] for n in range(8)) for side in (OWN, LEFT, RIGHT)]
+    fields = [sum(fpin[side, n] for n in range(8)) for side in (OWN, NEAR, FAR)]
     cfield = fields[OWN]
 
     def induce_part(step_no, side, acc):
@@ -215,12 +214,10 @@
             at = pl.ds(i * 8, 8)
             m = mucol[side, at, :]
             m = [m[:, a : a + 1] for a in range(3)]
-            t = [tens[side, n, at, :] for n in range(6)]
-            return (
-                acc[0] + (t[0] * m[0] + t[3] * m[1] + t[4] * m[2]),
-                acc[1] + (t[3] * m[0] + t[1] * m[1] + t[5] * m[2]),
-                acc[2] + (t[4] * m[0] + t[5] * m[1] + t[2] * m[2]),
-            )
+            f = [tens[side, a, at, :] for a in range(3)]
+            flat = tens[side, 3, at, :]
+            along = f[0] * m[0] + f[1] * m[1] + f[2] * m[2]
+            return tuple(acc[a] + (f[a] * along - flat * m[a]) for a in range(3))
 
         return lax.fori_loop(0, atoms // 8, step, acc, unroll=atoms // 8)
 
@@ -232,11 +229,12 @@
         mucol[side] = wide.T
 
     def rows_of(acc):
-        return jnp.concatenate([jnp.sum(acc[a], axis=0, keepdims=True) for a in range(3)], 0)
+        total = jnp.concatenate([jnp.sum(acc[a], axis=0, keepdims=True) for a in range(3)], 0)
+        return total * (3.0 / (CUT2 * CUT2))
 
     def induce_first():
         acc = (zero, zero, zero)
-        for side in (OWN, LEFT, RIGHT):
+        for side in (OWN, NEAR, FAR):
             columns(pk[side, 15:16, :] * fields[side], side)
             acc = induce_part(0, side, acc)
         return rows_of(acc)
@@ -244,10 +242,10 @@
     def induce(n, moment):
         mu[n, OWN] = moment
         copies = [
-            remote(mu.at[n, OWN], mu.at[n, RIGHT], mu_send.at[n, 0], mu_recv.at[n, 0], mu_left),
-            remote(mu.at[n, OWN], mu.at[n, LEFT], mu_send.at[n, 1], mu_recv.at[n, 1], mu_right),
+            remote(mu.at[n, OWN], mu.at[n, NEAR], mu_send.at[n, 0], mu_recv.at[n, 0], to_near),
+            remote(mu.at[n, OWN], mu.at[n, FAR], mu_send.at[n, 1], mu_recv.at[n, 1], mu_far),
         ]
-        for c in copies:
+        for c in copies[::-1]:
             c.start()
         mu_copies.extend(copies)
         if n == ITERS:
@@ -258,7 +256,7 @@
 
         columns(moment, OWN)
         acc = induce_part(n, OWN, (zero, zero, zero))
-        for c, side in zip(copies, (RIGHT, LEFT)):
+        for c, side in zip(copies, (NEAR, FAR)):
             c.wait_recv()
             columns(mu[n, side], side)
             acc = induce_part(n, side, acc)
@@ -314,6 +312,7 @@
                 pltpu.VMEM((3, beads, atoms), f32),
                 pltpu.VMEM((atoms,), f32), pltpu.VMEM((atoms,), f32), pltpu.VMEM((atoms,), jnp.int32),
                 dma((4,)),
+                pltpu.SemaphoreType.REGULAR,
                 pltpu.VMEM((3, 16, atoms), f32),
                 pltpu.VMEM((3, atoms, 16), f32),
                 pltpu.VMEM((beads, 3, 8, atoms), f32),
@@ -323,7 +322,7 @@
                 pltpu.VMEM((3, 8, 3, atoms), f32),
                 pltpu.VMEM((3, 8, atoms), f32),
                 pltpu.VMEM((3, atoms, 8), f32),
-                pltpu.VMEM((3, 6, atoms, atoms), f32),
+                pltpu.VMEM((3, 4, atoms, atoms), f32),
                 pltpu.VMEM((rounds, 3, 3, atoms), f32),
                 pltpu.VMEM((3, atoms, 8), f32),
                 pltpu.VMEM((3, atoms), f32),

time: 48.3 us -> 45.6 us (0.944)
  Pallas kernels: 45.4 us -> 42.8 us
    pallas_call x1, Pallas kernels: 45.4 us -> 42.8 us  [body(): pl.pallas_call(functools.partial(kernel, beads, atoms, spaces), out_shape...]
where the time goes in v2:
time: 45.6 us; the launch traced here: 45.4 us
  Pallas kernels  42.8 us (94%)
  local copies, waits for them, and re-layouts  1.95 us (4%)
  between operations  0.65 us (1%)
    pallas_call x1, Pallas kernels, body(): pl.pallas_call(functools.partial(kernel, beads, atoms, spaces), out_shape...  42.8 us
    unnamed x4, local copies, waits for them, and re-layouts  1.95 us

profile of v2, /device:TPU:2, one launch (start us, length us, event | category | flops | bytes accessed | tf_op | source)
XLA Modules:
  0.0 45.4 jit_solution(60274864861303733)
XLA Ops:
  0.6 42.8 %polarize.1 = (f32[3,4,384]{2,1,0:T(4,128)}, f32[3,4,384]{2,1,0:T(4,128)}) custom-call(f32[3,4,384]{2,1,0:T(4,128)} %bitcast.3, f32[384]{0:T(512)} %charge_hbm.1, f32[384]{0:T(512)} %polar_hbm.1, s32[384]{0:T(512)} %mol_hbm.1), custom_call_target="tpu_custom_call" | custom-call | tf_op jit(solution)/shard_map/polarize/pallas_call | solution.py:303
  43.4 0.0 copy-start
  43.4 1.3 %copy.8 = f32[4,3,384]{2,0,1:T(4,128)} copy(f32[4,3,384]{2,0,1:T(4,128)} %bitcast.5) | data formatting | bytes 36864
  44.8 0.0 copy-done
  44.8 0.6 %copy.9 = f32[4,3,384]{2,0,1:T(4,128)} copy(f32[4,3,384]{2,0,1:T(4,128)S(1)} %bitcast.4) | data formatting | bytes 36864
Async XLA Ops:
  43.4 1.3 %copy-start = (f32[3,4,384]{2,1,0:T(4,128)S(1)}, f32[3,4,384]{2,1,0:T(4,128)}, u32[]{:S(2)}) copy-start(f32[3,4,384]{2,1,0:T(4,128)} %get-tuple-element.5) | copy-start | bytes 55300

commit v3 on v2

--- a/solution.py
+++ b/solution.py
@@ -336,11 +336,14 @@
                 dma((4,)), dma((4,)),
             ],
             compiler_params=pltpu.CompilerParams(
-                collective_id=0, has_side_effects=True, vmem_limit_bytes=60 * 1024 * 1024
+                collective_id=0, has_side_effects=True, vmem_limit_bytes=40 * 1024 * 1024
             ),
             name="polarize",
         )(
-            positions.transpose(1, 0, 2), charges, polar, molecule
+            *[
+                pltpu.with_memory_space_constraint(x, pltpu.HBM)
+                for x in (positions.transpose(1, 0, 2), charges, polar, molecule)
+            ]
         )
         return total.transpose(1, 0, 2), moment.transpose(1, 0, 2)
 

time: 45.6 us -> 44.2 us (0.969)
  local copies, waits for them, and re-layouts: 1.95 us -> 1.21 us
  Pallas kernels: 42.8 us -> 42.2 us
    unnamed x4 -> x2, local copies, waits for them, and re-layouts: 1.95 us -> 1.21 us
    pallas_call x1, Pallas kernels: 42.8 us -> 42.2 us  [body(): pl.pallas_call(functools.partial(kernel, beads, atoms, spaces), out_shape...]
where the time goes in v3:
time: 44.2 us; the launch traced here: 44 us
  Pallas kernels  42.2 us (95%)
  local copies, waits for them, and re-layouts  1.21 us (3%)
  between operations  0.64 us (1%)
    pallas_call x1, Pallas kernels, body(): pl.pallas_call(functools.partial(kernel, beads, atoms, spaces), out_shape...  42.2 us
    unnamed x2, local copies, waits for them, and re-layouts  1.21 us

profile of v3, /device:TPU:2, one launch (start us, length us, event | category | flops | bytes accessed | tf_op | source)
XLA Modules:
  0.0 44.0 jit_solution(10738124325163708103)
XLA Ops:
  0.6 42.2 %polarize.1 = (f32[3,4,384]{2,1,0:T(4,128)S(1)}, f32[3,4,384]{2,1,0:T(4,128)S(1)}) custom-call(f32[3,4,384]{2,1,0:T(4,128)} %bitcast.5, f32[384]{0:T(512)} %charge_hbm.1, f32[384]{0:T(512)} %polar_hbm.1, s32[384]{0:T(512)} %mol_hbm.1), custom_call_target="tpu_custom_call" | custom-call | tf_op jit(solution)/shard_map/polarize/pallas_call | solution.py:303
  42.8 0.6 %copy.8 = f32[4,3,384]{2,0,1:T(4,128)} copy(f32[4,3,384]{2,0,1:T(4,128)S(1)} %bitcast.4) | data formatting | bytes 36864
  43.4 0.6 %copy.9 = f32[4,3,384]{2,0,1:T(4,128)} copy(f32[4,3,384]{2,0,1:T(4,128)S(1)} %bitcast.3) | data formatting | bytes 36864

commit v4 on v3

--- a/solution.py
+++ b/solution.py
@@ -47,7 +47,7 @@
         return ((half if turn == 0 else 1 - half) * 4 + lax.rem(spot + dx, 4), slabs[side])
 
     others = [(turn, dx) for turn in (1, 0) for dx in (2, 1, 3, 0) if (turn, dx) != (0, 0)]
-    around = [(turn, dx, side) for turn in (1, 0) for dx in (2, 1, 3, 0) for side in (FAR, NEAR, OWN)]
+    around = [(turn, dx, side) for side in (OWN, NEAR, FAR) for turn in (1, 0) for dx in (2, 1, 3, 0)]
     around.remove((0, 0, OWN))
     barrier = pltpu.get_barrier_semaphore()
     greeted = [peer(1, 0), peer(1, 0, NEAR), peer(1, 0, FAR), to_near, to_far]
@@ -140,13 +140,17 @@
             for a in range(3):
                 perm[l, a] = acc[a]
 
-    perm_from(NEAR)
-    halo[1].wait_recv()
-    for side in (OWN, NEAR, FAR):
+    def contract_spots(side):
         for a in range(3):
             spots = [pk[side, 4 * a + l : 4 * a + l + 1, :] for l in range(beads)]
             for dx in range(4):
                 cps[dx, side, a : a + 1, :] = sum(fold[dx][l] * spots[l] for l in range(beads))
+
+    perm_from(NEAR)
+    contract_spots(OWN)
+    contract_spots(NEAR)
+    halo[1].wait_recv()
+    contract_spots(FAR)
     pl.semaphore_wait(ready, len(row))
     sends = []
     for n, (turn, dx) in enumerate(others):
@@ -203,12 +207,6 @@
 
         lax.fori_loop(0, atoms // 8, step, 0, unroll=atoms // 8)
 
-    for c in fp_copies:
-        c.wait_recv()
-    fpin[OWN, 0] = fps[0]
-    fields = [sum(fpin[side, n] for n in range(8)) for side in (OWN, NEAR, FAR)]
-    cfield = fields[OWN]
-
     def induce_part(step_no, side, acc):
         def step(i, acc):
             at = pl.ds(i * 8, 8)
@@ -232,12 +230,20 @@
         total = jnp.concatenate([jnp.sum(acc[a], axis=0, keepdims=True) for a in range(3)], 0)
         return total * (3.0 / (CUT2 * CUT2))
 
-    def induce_first():
-        acc = (zero, zero, zero)
-        for side in (OWN, NEAR, FAR):
-            columns(pk[side, 15:16, :] * fields[side], side)
-            acc = induce_part(0, side, acc)
-        return rows_of(acc)
+    def cfield_of(side):
+        parts = [fps[0]] if side == OWN else []
+        for c, (turn, dx, at) in zip(fp_copies, around):
+            if at == side:
+                c.wait_recv()
+                parts.append(fpin[side, turn * 4 + dx])
+        return sum(parts)
+
+    cfield = cfield_of(OWN)
+    columns(alpha * cfield, OWN)
+    first = induce_part(0, OWN, (zero, zero, zero))
+    for side in (NEAR, FAR):
+        columns(pk[side, 15:16, :] * cfield_of(side), side)
+        first = induce_part(0, side, first)
 
     def induce(n, moment):
         mu[n, OWN] = moment
@@ -262,7 +268,7 @@
             acc = induce_part(n, side, acc)
         return rows_of(acc)
 
-    moment = alpha * (cfield + induce_first())
+    moment = alpha * (cfield + rows_of(first))
     for n in range(1, ITERS):
         moment = alpha * (cfield + induce(n, moment))
     ind[...] = induce(ITERS, moment)

time: 44.2 us -> 44.5 us (level)
  no operation moved by 1% of the time
where the time goes in v4:
time: 44.5 us; the launch traced here: 44.3 us
  Pallas kernels  42.4 us (95%)
  local copies, waits for them, and re-layouts  1.21 us (3%)
  between operations  0.64 us (1%)
    pallas_call x1, Pallas kernels, body(): pl.pallas_call(functools.partial(kernel, beads, atoms, spaces), out_shape...  42.4 us
    unnamed x2, local copies, waits for them, and re-layouts  1.21 us

profile of v4, /device:TPU:2, one launch (start us, length us, event | category | flops | bytes accessed | tf_op | source)
XLA Modules:
  0.0 44.3 jit_solution(15893380504902561236)
XLA Ops:
  0.6 42.4 %polarize.1 = (f32[3,4,384]{2,1,0:T(4,128)S(1)}, f32[3,4,384]{2,1,0:T(4,128)S(1)}) custom-call(f32[3,4,384]{2,1,0:T(4,128)} %bitcast.5, f32[384]{0:T(512)} %charge_hbm.1, f32[384]{0:T(512)} %polar_hbm.1, s32[384]{0:T(512)} %mol_hbm.1), custom_call_target="tpu_custom_call" | custom-call | tf_op jit(solution)/shard_map/polarize/pallas_call | solution.py:309
  43.1 0.6 %copy.8 = f32[4,3,384]{2,0,1:T(4,128)} copy(f32[4,3,384]{2,0,1:T(4,128)S(1)} %bitcast.4) | data formatting | bytes 36864
  43.7 0.6 %copy.9 = f32[4,3,384]{2,0,1:T(4,128)} copy(f32[4,3,384]{2,0,1:T(4,128)S(1)} %bitcast.3) | data formatting | bytes 36864
